TPU v7x, 32 devices: a whole 2x2x4 slice. The times are simulated.
32 devices in a mesh: dp: 8 (over z, x), tensor: 4 (over y, core).
Axes of the slice: x: 2, y: 2, z: 4, core: 2. Of those that a mesh axis runs over, the one named last changes fastest.
Arguments:
- inputs: bfloat16 [4096, 768], P(('dp', 'tensor')), may hold values from -6 to 6
- segment_ids: int32 [8, 512], P('dp'), may hold values from 0 to 3, never falling along the last dimension, each value on 1 to 256 neighbouring positions
- gain_attn: float32 [768], replicated, may hold values from 0.5 to 1.5
- gain_ffn: float32 [768], replicated, may hold values from 0.5 to 1.5
- query_key_value_weight: bfloat16 [768, 3, 768], P('dp', None, 'tensor'), may hold values from -1 to 1
- w_out: bfloat16 [768, 768], P('dp', 'tensor'), may hold values from -1.75 to 1.75
- w_ffn_in: bfloat16 [768, 2, 1152], P('dp', None, 'tensor'), may hold values from -0.21875 to 0.21875
- w_ffn_out: bfloat16 [768, 1152], P('dp', 'tensor'), may hold values from -0.1875 to 0.1875
- cotangent: bfloat16 [4096, 768], P(('dp', 'tensor')), may hold values from -6 to 6
Outputs:
- output: bfloat16 [4096, 768], P(('dp', 'tensor'))
- input_grad: float32 [4096, 768], P(('dp', 'tensor'))
- gain_attn_grad: float32 [768], replicated
- gain_ffn_grad: float32 [768], replicated
- w_qkv_grad: float32 [768, 3, 768], P('dp', None, 'tensor')
- w_out_grad: float32 [768, 768], P('dp', 'tensor')
- w_ffn_in_grad: float32 [768, 2, 1152], P('dp', None, 'tensor')
- w_ffn_out_grad: float32 [768, 1152], P('dp', 'tensor')
Inputs may be any that keep to these rules, and one draw needn't show every extreme that they name: `segment_ids`: each row holds the sequence numbers of one data group's 512 tokens: 4 whole sequences laid end to end, numbers never falling, each sequence 1 to 256 tokens long and one exactly 256.
All inputs are finite; a program needn't handle non-finite values.
Results may differ from a plain program's by a relative error of at most 0.013.
Values may be sent and summed in bfloat16 or wider, within the bound.
A program may use at most 64 MiB of HBM per device.

v0:
```python
import jax
import jax.numpy as jnp
from jax import lax
from jax.sharding import PartitionSpec as P

HD = 64


EPS = 1e-05
THETA = 160000.0


def normalize(row_data):
    centre = row_data - jnp.mean(row_data, axis=-1, keepdims=True)
    inverse = lax.rsqrt(jnp.mean(centre * centre, axis=-1, keepdims=True) + EPS)
    return (centre * inverse, inverse)


def norm_back(grad_normed, unit_rows, inverse, gain_row):
    grad_unit = grad_normed * gain_row
    mean_grad = jnp.mean(grad_unit, axis=-1, keepdims=True)
    mean_dot = jnp.mean(grad_unit * unit_rows, axis=-1, keepdims=True)
    return inverse * (grad_unit - mean_grad - unit_rows * mean_dot)


def gelu_parts(values_in):
    normal_cdf = 0.5 * (1.0 + jax.scipy.special.erf(values_in * 0.7071067811865476))
    density = 0.3989422804014327 * jnp.exp(-0.5 * values_in * values_in)
    return (values_in * normal_cdf, normal_cdf + values_in * density)


def rotary_tables(segments, head_size):
    token_count = segments.shape[0]
    places = jnp.arange(token_count, dtype=jnp.int32)
    previous = jnp.concatenate([jnp.full((1,), -1, jnp.int32), segments[:-1]])
    starts = lax.cummax(jnp.where(segments != previous, places, 0), axis=0)
    position = (places - starts).astype(jnp.float32)
    half_size = head_size // 2
    exponent = -(2.0 * jnp.arange(half_size, dtype=jnp.float32)) / head_size
    frequency = jnp.power(jnp.float32(THETA), exponent)
    angles = position[:, None] * frequency[None, :]
    return (jnp.cos(angles), jnp.sin(angles))


def rotate(vectors, cosine, sine):
    half_size = vectors.shape[-1] // 2
    first_half = vectors[..., :half_size]
    second_half = vectors[..., half_size:]
    cos_part = cosine[:, None, :]
    sin_part = sine[:, None, :]
    return jnp.concatenate(
        [
            first_half * cos_part - second_half * sin_part,
            second_half * cos_part + first_half * sin_part,
        ],
        axis=-1,
    )


def block_scores(q_block, keyset, seg_block, segments, scale):
    scores = jnp.einsum("qhe,khe->hqk", q_block, keyset, preferred_element_type=jnp.float32) * scale
    same_seq = seg_block[:, None] == segments[None, :]
    return jnp.where(same_seq[None], scores, jnp.float32(-1e30))


def attention_forward(query, keyset, valueset, segments):
    scale = query.shape[-1] ** (-0.5)
    scores = block_scores(query, keyset, segments, segments, scale)
    top_score = jnp.max(scores, axis=-1, keepdims=True)
    log_total = top_score + jnp.log(jnp.sum(jnp.exp(scores - top_score), axis=-1, keepdims=True))
    probs = jnp.exp(scores - log_total).astype(jnp.bfloat16)
    out_block = jnp.einsum("hqk,khe->qhe", probs, valueset, preferred_element_type=jnp.float32)
    out_list = out_block.astype(jnp.bfloat16)
    return (out_list, log_total)


def attention_backward(query, keyset, valueset, segments, heads_out, log_totals, grad_heads):
    scale = query.shape[-1] ** (-0.5)
    scores = block_scores(query, keyset, segments, segments, scale)
    probs_f = jnp.exp(scores - log_totals)
    probs = probs_f.astype(jnp.bfloat16)
    grad_values = jnp.einsum("hqk,qhe->khe", probs, grad_heads, preferred_element_type=jnp.float32)
    grad_probs = jnp.einsum(
        "qhe,khe->hqk", grad_heads, valueset, preferred_element_type=jnp.float32
    )
    row_dot = jnp.sum(grad_heads.astype(jnp.float32) * heads_out.astype(jnp.float32), axis=-1).T[
        :, :, None
    ]
    grad_scores = (probs_f * (grad_probs - row_dot)).astype(jnp.bfloat16)
    query_list = (
        jnp.einsum("hqk,khe->qhe", grad_scores, keyset, preferred_element_type=jnp.float32) * scale
    )
    grad_keys = (
        jnp.einsum("hqk,qhe->khe", grad_scores, query, preferred_element_type=jnp.float32) * scale
    )
    return (query_list, grad_keys, grad_values)


def spread_rows(row_data):
    return lax.all_gather(row_data, "tensor", axis=0, tiled=True)


def merge_rows(partial_value):
    return lax.psum_scatter(partial_value, "tensor", scatter_dimension=0, tiled=True)


def spread_grads(row_data):
    return lax.all_gather(row_data, "tensor", axis=0, tiled=True)


def merge_grads(partial_value):
    return lax.psum_scatter(partial_value, "tensor", scatter_dimension=0, tiled=True)


def on_device(
    inputs,
    segment_ids,
    gain_attn,
    gain_ffn,
    query_key_value_weight,
    w_out,
    w_ffn_in,
    w_ffn_out,
    cotangent,
):
    query_key_value_full, full_out, full_in, full_down = (
        lax.all_gather(query_key_value_weight, "dp", axis=0, tiled=True),
        lax.all_gather(w_out, "dp", axis=0, tiled=True),
        lax.all_gather(w_ffn_in, "dp", axis=0, tiled=True),
        lax.all_gather(w_ffn_out, "dp", axis=0, tiled=True),
    )
    seg_row = segment_ids[0]
    token_count = seg_row.shape[0]
    contract_last = (((1,), (1,)), ((), ()))
    contract_first = (((0,), (0,)), ((), ()))
    resid_in = inputs.astype(jnp.float32)
    unit_one, inv_one = normalize(resid_in)
    first_normed_rows = spread_rows((unit_one * gain_attn).astype(jnp.bfloat16))
    attention_mixed = jnp.einsum(
        "jk,knr->jnr", first_normed_rows, query_key_value_full, preferred_element_type=jnp.float32
    )
    cosine, sine = rotary_tables(seg_row, HD)
    query = rotate(attention_mixed[:, 0].reshape(token_count, -1, HD), cosine, sine).astype(
        jnp.bfloat16
    )
    keyset = rotate(attention_mixed[:, 1].reshape(token_count, -1, HD), cosine, sine).astype(
        jnp.bfloat16
    )
    valueset = attention_mixed[:, 2].reshape(token_count, -1, HD).astype(jnp.bfloat16)
    heads_out, log_totals = attention_forward(query, keyset, valueset, seg_row)
    flat_out = heads_out.reshape(token_count, -1)
    attn_part = lax.dot_general(
        flat_out, full_out, contract_last, preferred_element_type=jnp.float32
    )
    resid_mid = resid_in + merge_rows(attn_part)
    unit_two, inv_two = normalize(resid_mid)
    normed_two = spread_rows((unit_two * gain_ffn).astype(jnp.bfloat16))
    gate_up = jnp.einsum("td,dsf->tsf", normed_two, full_in, preferred_element_type=jnp.float32)
    gelu_val, gelu_slope = gelu_parts(gate_up[:, 0])
    hidden = (gelu_val * gate_up[:, 1]).astype(jnp.bfloat16)
    ffn_part = lax.dot_general(hidden, full_down, contract_last, preferred_element_type=jnp.float32)
    result = (resid_mid + merge_rows(ffn_part)).astype(jnp.bfloat16)
    query_key_value_back, back_out, back_in, back_down = (
        query_key_value_full,
        full_out,
        full_in,
        full_down,
    )
    grad_top = spread_grads(cotangent)
    down_grad = lax.dot_general(
        grad_top, hidden, contract_first, preferred_element_type=jnp.float32
    )
    grad_hidden = jnp.dot(grad_top, back_down, preferred_element_type=jnp.float32)
    grad_mix = jnp.stack(
        [grad_hidden * gate_up[:, 1] * gelu_slope, grad_hidden * gelu_val], axis=1
    ).astype(jnp.bfloat16)
    in_grad = jnp.einsum("td,tsf->dsf", normed_two, grad_mix, preferred_element_type=jnp.float32)
    grad_two = merge_grads(
        jnp.einsum("tsf,dsf->td", grad_mix, back_in, preferred_element_type=jnp.float32)
    )
    gain_ffn_part = jnp.sum(grad_two * unit_two, axis=0)
    grad_mid = cotangent.astype(jnp.float32) + norm_back(grad_two, unit_two, inv_two, gain_ffn)
    grad_mid_full = spread_grads(grad_mid.astype(jnp.bfloat16))
    out_grad = lax.dot_general(
        grad_mid_full, flat_out, contract_first, preferred_element_type=jnp.float32
    )
    grad_heads = jnp.dot(grad_mid_full, back_out, preferred_element_type=jnp.float32).astype(
        jnp.bfloat16
    )
    grad_heads = grad_heads.reshape(token_count, -1, HD)
    grad_query, grad_keys, grad_values = attention_backward(
        query, keyset, valueset, seg_row, heads_out, log_totals, grad_heads
    )
    grad_query = rotate(grad_query, cosine, -sine)
    grad_keys = rotate(grad_keys, cosine, -sine)
    query_key_value_gradient = jnp.stack(
        [
            grad_query.reshape(token_count, -1),
            grad_keys.reshape(token_count, -1),
            grad_values.reshape(token_count, -1),
        ],
        axis=1,
    ).astype(jnp.bfloat16)
    gradient_query_key_value = jnp.einsum(
        "hz,hjx->zjx",
        first_normed_rows,
        query_key_value_gradient,
        preferred_element_type=jnp.float32,
    )
    first_norm_gradient = merge_grads(
        jnp.einsum(
            "bwi,uwi->bu",
            query_key_value_gradient,
            query_key_value_back,
            preferred_element_type=jnp.float32,
        )
    )
    gain_attn_part = jnp.sum(first_norm_gradient * unit_one, axis=0)
    grad_input = grad_mid + norm_back(first_norm_gradient, unit_one, inv_one, gain_attn)
    gain_attn_grad, gain_ffn_grad = lax.psum((gain_attn_part, gain_ffn_part), ("dp", "tensor"))
    qkv_share, out_share, in_share, down_share = (
        lax.psum_scatter(gradient_query_key_value, "dp", scatter_dimension=0, tiled=True),
        lax.psum_scatter(out_grad, "dp", scatter_dimension=0, tiled=True),
        lax.psum_scatter(in_grad, "dp", scatter_dimension=0, tiled=True),
        lax.psum_scatter(down_grad, "dp", scatter_dimension=0, tiled=True),
    )
    return (
        result,
        grad_input,
        gain_attn_grad,
        gain_ffn_grad,
        qkv_share,
        out_share,
        in_share,
        down_share,
    )


def solution(mesh):
    return jax.shard_map(
        on_device,
        mesh=mesh,
        in_specs=(
            P(("dp", "tensor"), None),
            P("dp", None),
            P(),
            P(),
            P("dp", None, "tensor"),
            P("dp", "tensor"),
            P("dp", None, "tensor"),
            P("dp", "tensor"),
            P(("dp", "tensor"), None),
        ),
        out_specs=(
            P(("dp", "tensor"), None),
            P(("dp", "tensor"), None),
            P(),
            P(),
            P("dp", None, "tensor"),
            P("dp", "tensor"),
            P("dp", None, "tensor"),
            P("dp", "tensor"),
        ),
        check_vma=False,
    )
```

profile of v0, /device:TPU:25, one launch (start us, length us, event | category | flops | bytes accessed | tf_op | source)
XLA Modules:
  0.0 557.2 jit_solution(11263449682308552029)
XLA Ops:
  8.3 1.1 fusion.31
  11.6 9.1 %all_gather.24 = bf16[512,768]{1,0:T(8,128)(2,1)S(1)} all-gather(bf16[128,768]{1,0:T(8,128)(2,1)S(1)} %fusion.25), channel_id=1, replica_groups=mesh['dp'=8,'tensor'=4] {'tensor'}, dimensions={0}, use_global_device_ids=true | all-gather | bytes 983040 | tf_op jit(solution)/shard_map/all_gather | solution.py:100
  20.7 31.9 %all_gather.25 = bf16[768,3,192]{2,1,0:T(4,128)(2,1)S(1)} all-gather(bf16[96,3,192]{2,1,0:T(4,128)(2,1)S(1)} %copy.43), channel_id=1, replica_groups=mesh['dp'=8,'tensor'=4] {'dp'}, dimensions={0}, use_global_device_ids=true | all-gather | bytes 995328 | tf_op jit(solution)/shard_map/all_gather | solution.py:127
  55.2 23.7 %all_gather.26 = bf16[768,192]{1,0:T(8,128)(2,1)S(1)} all-gather(bf16[96,192]{1,0:T(8,128)(2,1)S(1)} %copy-done.38), channel_id=1, replica_groups=mesh['dp'=8,'tensor'=4] {'dp'}, dimensions={0}, use_global_device_ids=true | all-gather | bytes 331776 | tf_op jit(solution)/shard_map/all_gather | solution.py:128
  83.2 1.6 fusion.51
  84.9 26.6 %all_gather.29 = bf16[768,288]{1,0:T(8,128)(2,1)} all-gather(bf16[96,288]{1,0:T(8,128)(2,1)S(1)} %copy-done.37), channel_id=1, replica_groups=mesh['dp'=8,'tensor'=4] {'dp'}, dimensions={0}, use_global_device_ids=true | all-gather | bytes 497664 | tf_op jit(solution)/shard_map/all_gather | solution.py:130
  111.5 25.9 %all_gather.30 = bf16[512,768]{1,0:T(8,128)(2,1)} all-gather(bf16[128,768]{1,0:T(8,128)(2,1)S(1)} %copy-done.15), channel_id=1, replica_groups=mesh['dp'=8,'tensor'=4] {'tensor'}, dimensions={0}, use_global_device_ids=true | all-gather | bytes 983040 | tf_op jit(solution)/shard_map/all_gather | solution.py:108
  137.4 28.4 %all_gather.28 = bf16[768,2,288]{2,1,0:T(2,128)(2,1)S(1)} all-gather(bf16[96,2,288]{2,1,0:T(2,128)(2,1)S(1)} %copy-done.36), channel_id=1, replica_groups=mesh['dp'=8,'tensor'=4] {'dp'}, dimensions={0}, use_global_device_ids=true | all-gather | bytes 995328 | tf_op jit(solution)/shard_map/all_gather | solution.py:129
  167.3 12.9 %all_gather.27 = bf16[512,768]{1,0:T(8,128)(2,1)S(1)} all-gather(bf16[128,768]{1,0:T(8,128)(2,1)S(1)} %multiply_convert_fusion.3), channel_id=1, replica_groups=mesh['dp'=8,'tensor'=4] {'tensor'}, dimensions={0}, use_global_device_ids=true | all-gather | bytes 983040 | tf_op jit(solution)/shard_map/all_gather | solution.py:100
  180.9 1.4 fusion.33
  183.1 2.0 convolution_bitcast_fusion.1
  185.2 3.0 fusion.52
  188.3 2.3 fusion.9
  190.7 23.6 %reduce-scatter.15.cloned.1.call-done = f32[128,768]{1,0:T(8,128)} async-done(((f32[512,768]{1,0:T(8,128)}), f32[128,768]{1,0:T(8,128)}) %reduce-scatter.15.cloned.1.call-update) | async-done | bytes 393232 | tf_op jit(solution)/shard_map/reduce_scatter | solution.py:112
  214.3 1.2 multiply_reduce_fusion
  215.6 29.5 %reduce-scatter.13.cloned.1.call-done = f32[128,768]{1,0:T(8,128)} async-done(((f32[512,768]{1,0:T(8,128)}), f32[128,768]{1,0:T(8,128)}) %reduce-scatter.13.cloned.1.call-update) | async-done | bytes 393232 | tf_op jit(solution)/shard_map/reduce_scatter | solution.py:104
  245.1 2.0 fusion.47
  247.1 8.9 %all_gather.31 = bf16[512,768]{1,0:T(8,128)(2,1)S(1)} all-gather(bf16[128,768]{1,0:T(8,128)(2,1)S(1)} %get-tuple-element.40), channel_id=1, replica_groups=mesh['dp'=8,'tensor'=4] {'tensor'}, dimensions={0}, use_global_device_ids=true | all-gather | bytes 983040 | tf_op jit(solution)/shard_map/all_gather | solution.py:108
  256.6 1.2 multiply_convert_fusion
  260.7 2.0 convolution_bitcast_fusion
  263.2 1.4 copy.66
  264.6 1.3 fusion.53
  266.1 2.2 fusion.7
  268.3 46.6 %reduce-scatter.23.cloned.1.call-done = f32[96,2,288]{2,0,1:T(8,128)} async-done(((f32[768,2,288]{2,0,1:T(8,128)}), f32[96,2,288]{2,0,1:T(8,128)}) %reduce-scatter.23.cloned.1.call-update) | async-done | bytes 221200 | tf_op jit(solution)/shard_map/reduce_scatter | solution.py:224
  314.9 1.9 copy.55
  316.8 30.9 %reduce-scatter.17.cloned.1.call-done = f32[128,768]{1,0:T(8,128)} async-done(((f32[512,768]{1,0:T(8,128)}), f32[128,768]{1,0:T(8,128)}) %reduce-scatter.17.cloned.1.call-update) | async-done | bytes 393232 | tf_op jit(solution)/shard_map/reduce_scatter | solution.py:112
  347.7 1.2 fusion.30
  349.0 38.5 %all-reduce = (f32[768]{0:T(1024)}, f32[768]{0:T(1024)}) all-reduce(f32[768]{0:T(1024)S(1)} %get-tuple-element.34, f32[768]{0:T(1024)S(1)} %get-tuple-element.32), channel_id=1, replica_groups=mesh['dp'=8,'tensor'=4] {'dp','tensor'}, use_global_device_ids=true, to_apply=%region_18.19 | all-reduce | flops 1536 | bytes 12288 | tf_op jit(solution)/shard_map/psum | solution.py:220
  387.4 1.9 fusion.29
  389.4 23.5 %reduce-scatter.25.cloned.1.call-done = f32[96,288]{1,0:T(8,128)} async-done(((f32[768,288]{1,0:T(8,128)}), f32[96,288]{1,0:T(8,128)}) %reduce-scatter.25.cloned.1.call-update) | async-done | bytes 110608
  412.8 65.3 %reduce-scatter.21.cloned.1.call-done = f32[96,192]{1,0:T(8,128)} async-done(((f32[768,192]{1,0:T(8,128)}), f32[96,192]{1,0:T(8,128)}) %reduce-scatter.21.cloned.1.call-update) | async-done | bytes 73744 | tf_op jit(solution)/shard_map/reduce_scatter | solution.py:223
  478.1 72.3 %reduce-scatter.19.cloned.1.call-done = f32[96,3,192]{2,0,1:T(8,128)} async-done(((f32[768,3,192]{2,0,1:T(8,128)}), f32[96,3,192]{2,0,1:T(8,128)}) %reduce-scatter.19.cloned.1.call-update) | async-done | bytes 221200 | tf_op jit(solution)/shard_map/reduce_scatter | solution.py:222
  (146 shorter events, 17.0 us)
Async XLA Ops:
  7.2 158.6 %reduce-scatter.11.cloned.1.call-start = ((), (), s32[]{:S(2)}) async-start(), calls=%async_computation.8 | async-start | bytes 1966080 | tf_op jit(solution)/shard_map/reduce_scatter | solution.py:104
  20.7 33.4 %copy-start.5 = (bf16[512,768]{1,0:T(8,128)(2,1)}, bf16[512,768]{1,0:T(8,128)(2,1)S(1)}, u32[]{:S(2)}) copy-start(bf16[512,768]{1,0:T(8,128)(2,1)S(1)} %all_gather.24) | copy-start | bytes 2359300
  54.2 27.3 %copy-start.30 = (bf16[512,1,192]{0,2,1:T(8,128)(2,1)}, bf16[512,1,192]{0,2,1:T(8,128)(2,1)S(1)}, u32[]{:S(2)}) copy-start(bf16[512,1,192]{0,2,1:T(8,128)(2,1)S(1)} %slice.128) | copy-start | bytes 589828
  55.2 26.4 %copy-start.13 = (pred[512,512]{0,1:T(8,128)(4,1)}, pred[512,512]{0,1:T(8,128)(4,1)S(1)}, u32[]{:S(2)}) copy-start(pred[512,512]{0,1:T(8,128)(4,1)S(1)} %broadcast_compare_fusion) | copy-start | bytes 786436
  78.9 3.7 copy-start.1
  82.5 2.3 copy-start.37
  82.5 29.0 %copy-start.15 = (bf16[128,768]{1,0:T(8,128)(2,1)S(1)}, bf16[128,768]{1,0:T(8,128)(2,1)}, u32[]{:S(2)}) copy-start(bf16[128,768]{1,0:T(8,128)(2,1)} %param.17) | copy-start | bytes 589828
  83.2 54.2 %copy-start.36 = (bf16[96,2,288]{2,1,0:T(2,128)(2,1)S(1)}, bf16[96,2,288]{2,1,0:T(2,128)(2,1)}, u32[]{:S(2)}) copy-start(bf16[96,2,288]{2,1,0:T(2,128)(2,1)} %param.15) | copy-start | bytes 331780
  84.8 81.0 %copy-start = (bf16[128,768]{1,0:T(8,128)(2,1)S(1)}, bf16[128,768]{1,0:T(8,128)(2,1)}, u32[]{:S(2)}) copy-start(bf16[128,768]{1,0:T(8,128)(2,1)} %param.9) | copy-start | bytes 589828
  84.8 82.3 %copy-start.39 = (f32[768]{0:T(1024)S(1)}, f32[768]{0:T(1024)}, u32[]{:S(2)}) copy-start(f32[768]{0:T(1024)} %param.12) | copy-start | bytes 9220
  84.8 129.5 %reduce-scatter.15.cloned.1.call-start = ((), (), s32[]{:S(2)}) async-start(), calls=%async_computation.10 | async-start | bytes 1966080 | tf_op jit(solution)/shard_map/reduce_scatter | solution.py:112
  167.1 13.8 %copy-start.7 = (bf16[512,768]{1,0:T(8,128)(2,1)S(1)}, bf16[512,768]{1,0:T(8,128)(2,1)}, u32[]{:S(2)}) copy-start(bf16[512,768]{1,0:T(8,128)(2,1)} %all_gather.30) | copy-start | bytes 2359300
  167.1 13.8 %copy-start.9 = (bf16[768,288]{1,0:T(8,128)(2,1)S(1)}, bf16[768,288]{1,0:T(8,128)(2,1)}, u32[]{:S(2)}) copy-start(bf16[768,288]{1,0:T(8,128)(2,1)} %all_gather.29) | copy-start | bytes 1327108
  185.1 3.2 copy-start.26
  185.2 3.2 copy-start.28
  185.2 59.9 %reduce-scatter.13.cloned.1.call-start = ((), (), s32[]{:S(2)}) async-start(), calls=%async_computation.9 | async-start | bytes 1966080 | tf_op jit(solution)/shard_map/reduce_scatter | solution.py:104
  188.3 126.6 %reduce-scatter.23.cloned.1.call-start = ((), (), s32[]{:S(2)}) async-start(), calls=%async_computation.14 | async-start | bytes 2654208 | tf_op jit(solution)/shard_map/reduce_scatter | solution.py:224
  190.6 54.5 %copy-start.16 = (bf16[128,768]{1,0:T(8,128)(2,1)S(1)}, bf16[128,768]{1,0:T(8,128)(2,1)}, u32[]{:S(2)}) copy-start(bf16[128,768]{1,0:T(8,128)(2,1)} %param.17) | copy-start | bytes 589828
  190.6 65.4 %copy-start.2 = (bf16[768,192]{1,0:T(8,128)(2,1)S(1)}, bf16[768,192]{1,0:T(8,128)(2,1)}, u32[]{:S(2)}) copy-start(bf16[768,192]{1,0:T(8,128)(2,1)} %copy-done.1) | copy-start | bytes 884740
  190.6 157.1 %reduce-scatter.17.cloned.1.call-start = ((), (), s32[]{:S(2)}) async-start(), calls=%async_computation.11 | async-start | bytes 1966080 | tf_op jit(solution)/shard_map/reduce_scatter | solution.py:112
  215.6 40.9 %copy-start.11 = (bf16[3,64,512]{2,1,0:T(8,128)(2,1)S(1)}, bf16[3,64,512]{2,1,0:T(8,128)(2,1)}, u32[]{:S(2)}) copy-start(bf16[3,64,512]{2,1,0:T(8,128)(2,1)} %copy-done.10) | copy-start | bytes 589828
  245.1 11.4 %copy-start.4 = (f32[3,512,512]{1,2,0:T(8,128)S(1)}, f32[3,512,512]{1,2,0:T(8,128)}, u32[]{:S(2)}) copy-start(f32[3,512,512]{1,2,0:T(8,128)} %copy-done.3) | copy-start | bytes 9437188
  245.1 11.4 %copy-start.14 = (pred[512,512]{0,1:T(8,128)(4,1)S(1)}, pred[512,512]{0,1:T(8,128)(4,1)}, u32[]{:S(2)}) copy-start(pred[512,512]{0,1:T(8,128)(4,1)} %copy-done.13) | copy-start | bytes 786436
  245.1 11.4 %copy-start.31 = (bf16[512,1,192]{0,2,1:T(8,128)(2,1)S(1)}, bf16[512,1,192]{0,2,1:T(8,128)(2,1)}, u32[]{:S(2)}) copy-start(bf16[512,1,192]{0,2,1:T(8,128)(2,1)} %copy-done.30) | copy-start | bytes 589828
  256.6 1.9 copy-start.18
  256.6 1.9 copy-start.20
  260.7 2.1 copy-start.8
  260.7 2.1 copy-start.12
  262.7 150.1 %reduce-scatter.25.cloned.1.call-start = ((), (), s32[]{:S(2)}) async-start(), calls=%async_computation.15 | async-start | bytes 1327104
  264.6 213.5 %reduce-scatter.21.cloned.1.call-start = ((), (), s32[]{:S(2)}) async-start(), calls=%async_computation.13 | async-start | bytes 884736 | tf_op jit(solution)/shard_map/reduce_scatter | solution.py:223
  266.0 284.4 %reduce-scatter.19.cloned.1.call-start = ((), (), s32[]{:S(2)}) async-start(), calls=%async_computation.12 | async-start | bytes 2654208 | tf_op jit(solution)/shard_map/reduce_scatter | solution.py:222
  268.3 79.4 %copy-start.40 = (f32[768]{0:T(1024)S(1)}, f32[768]{0:T(1024)}, u32[]{:S(2)}) copy-start(f32[768]{0:T(1024)} %param.11) | copy-start | bytes 9220
  (20 other events, 24.7 us)
Sparse Core Ops, SparseCore 0:
  84.9 39.5 reduce-scatter.10
  185.3 29.0 reduce-scatter.14
  216.9 28.1 reduce-scatter.12
  248.8 66.0 reduce-scatter.22
  317.4 30.2 reduce-scatter.16
  351.5 61.2 reduce-scatter.24
  416.7 61.3 reduce-scatter.20
  482.6 67.7 reduce-scatter.18
where the time goes:
time: 563 us; the launch traced here: 557 us
  waiting for transfers between devices  292 us (52%)
  blocking collectives  206 us (37%)
  matrix products  22.8 us (4%)
  between operations  14.8 us (3%)
  other arithmetic  13.8 us (2%)
  local copies, waits for them, and re-layouts  7.78 us (1%)
    reduce_scatter x1, waiting for transfers between devices, on_device(): lax.psum_scatter(gradient_query_key_value, 'dp', scatter_dimension=0, til...  72.3 us
    reduce_scatter x1, waiting for transfers between devices, on_device(): lax.psum_scatter(out_grad, 'dp', scatter_dimension=0, tiled=True)  65.3 us
    reduce_scatter x2, waiting for transfers between devices, merge_grads(): lax.psum_scatter(partial_value, 'tensor', scatter_dimension=0, tiled=True)  54.6 us
    reduce_scatter x1, waiting for transfers between devices, on_device(): lax.psum_scatter(in_grad, 'dp', scatter_dimension=0, tiled=True)  46.6 us
    psum x1, blocking collectives, on_device(): lax.psum((gain_attn_part, gain_ffn_part), ('dp', 'tensor'))  38.5 us
    all_gather x2, blocking collectives, spread_grads(): return lax.all_gather(row_data, 'tensor', axis=0, tiled=True)  34.8 us
    all_gather x1, blocking collectives, on_device(): lax.all_gather(query_key_value_weight, 'dp', axis=0, tiled=True)  31.9 us
    reduce_scatter x2, waiting for transfers between devices, merge_rows(): lax.psum_scatter(partial_value, 'tensor', scatter_dimension=0, tiled=True)  29.5 us
  transfers between devices with their start and end apart: 8, of which 7 were waited for; matrix products, arithmetic and copies ran while one was open for 4% of the time, Pallas kernels for 0%

commit v1 on v0

--- a/solution.py
+++ b/solution.py
@@ -1,6 +1,11 @@
+import functools
+
 import jax
 import jax.numpy as jnp
+import numpy as np
 from jax import lax
+from jax.experimental import pallas as pl
+from jax.experimental.pallas import tpu as pltpu
 from jax.sharding import PartitionSpec as P
 
 HD = 64
@@ -236,9 +241,450 @@
     )
 
 
+BF = jnp.bfloat16
+F32 = jnp.float32
+LAST = (((1,), (1,)), ((), ()))
+FIRST = (((0,), (0,)), ((), ()))
+PLAIN = (((1,), (0,)), ((), ()))
+
+
+def dot(a, b, dims=PLAIN):
+    return lax.dot_general(a, b, dims, preferred_element_type=F32)
+
+
+def partner(chunk):
+    lane = lax.broadcasted_iota(jnp.int32, chunk.shape, 1)
+    return jnp.where(lane % 64 < 32, pltpu.roll(chunk, 96, 1), pltpu.roll(chunk, 32, 1))
+
+
+def rms_parts(rows):
+    centre = rows - jnp.mean(rows, axis=-1, keepdims=True)
+    inverse = lax.rsqrt(jnp.mean(centre * centre, axis=-1, keepdims=True) + EPS)
+    return centre * inverse, inverse
+
+
+def fused_kernel(
+    n_dp, n_t, n_head, ff,
+    x_ref, cot_ref, seg_ref, gain1_ref, gain2_ref, freq_ref, a_ref, b_ref,
+    out_ref, gin_ref, gains_ref, ga_ref, gb_ref,
+    xg, cg, ag, bg, n1, n2g, gmg, cosb, sinb, bias, qkvh, probs, hoh, hof, wo, wg, wu, wd,
+    rs1s, rs1r, rs2s, rs2r, rs3s, rs3r, rs4s, rs4r, own1, own2, own3, own4,
+    ghf, hid, mix0, mix1, unit2, mid, gmid, ghh, dsb, dqkv, gq, ags, agr, bgs, bgr, gpt, gpd,
+    t_send, t_recv, d_send, d_recv,
+):
+    d = lax.axis_index("dp")
+    t = lax.axis_index("tensor")
+    rows, width = x_ref.shape
+    wrows = a_ref.shape[0]
+    head_cols = n_head * HD
+    qkv_cols = 3 * head_cols
+    span = n_t * rows
+
+    barrier = pltpu.get_barrier_semaphore()
+    for o in range(1, n_t):
+        pl.semaphore_signal(barrier, inc=1, device_id=(d, lax.rem(t + o, n_t)), device_id_type=pl.DeviceIdType.MESH)
+    for o in range(1, n_dp):
+        pl.semaphore_signal(barrier, inc=1, device_id=(lax.rem(d + o, n_dp), t), device_id_type=pl.DeviceIdType.MESH)
+    pl.semaphore_wait(barrier, n_t + n_dp - 2)
+
+    def t_copy(stage, src, dst, to, slot):
+        return pltpu.make_async_remote_copy(
+            src_ref=src, dst_ref=dst, send_sem=t_send.at[stage, to], recv_sem=t_recv.at[stage, slot],
+            device_id=(d, to), device_id_type=pl.DeviceIdType.MESH)
+
+    def d_copy(stage, src, dst, to, slot):
+        return pltpu.make_async_remote_copy(
+            src_ref=src, dst_ref=dst, send_sem=d_send.at[stage, to], recv_sem=d_recv.at[stage, slot],
+            device_id=(to, t), device_id_type=pl.DeviceIdType.MESH)
+
+    def t_spread(stage, src, buf):
+        for o in (2, 3, 1)[: n_t - 1]:
+            t_copy(stage, src, buf.at[t], lax.rem(t + o, n_t), t).start()
+
+    def t_got(stage, buf, p):
+        t_copy(stage, buf.at[p], buf.at[p], p, p).wait_recv()
+
+    def d_got(stage, buf, p):
+        d_copy(stage, buf, buf, p, p).wait_recv()
+
+    def wslice(p):
+        return pl.ds(pl.multiple_of(p * wrows, 16), wrows)
+
+    t_spread(0, x_ref, xg)
+    for o in range(1, n_dp):
+        d_copy(0, a_ref, ag.at[wslice(d)], lax.rem(d + o, n_dp), d).start()
+    t_spread(1, cot_ref, cg)
+    for o in range(1, n_dp):
+        d_copy(1, b_ref, bg.at[wslice(d)], lax.rem(d + o, n_dp), d).start()
+    xg[t] = x_ref[...]
+    cg[t] = cot_ref[...]
+    ag[wslice(d), :] = a_ref[...]
+    bg[wslice(d), :] = b_ref[...]
+
+    segs = seg_ref[...].astype(F32)
+    seg_all = jnp.broadcast_to(segs, (rows, span))
+    lane_s = lax.broadcasted_iota(jnp.int32, (rows, span), 1)
+    row_s = lax.broadcasted_iota(jnp.int32, (rows, span), 0)
+    lane_p = lax.broadcasted_iota(jnp.int32, (rows, 128), 1)
+    sign = jnp.where(lane_p % 64 < 32, -1.0, 1.0).astype(F32)
+
+    def table_step(j, c):
+        place = row_s + j * rows
+        column = jnp.sum(jnp.where(lane_s == place, seg_all, 0.0), axis=1, keepdims=True)
+        same = seg_all == column
+        bias[j] = jnp.where(same, 0.0, -1e30).astype(F32)
+        position = jnp.sum(jnp.where(same & (lane_s < place), 1.0, 0.0), axis=1, keepdims=True)
+        angle = position * freq_ref[...]
+        cosb[j] = jnp.cos(angle)
+        sinb[j] = jnp.sin(angle) * sign
+        return c
+
+    lax.fori_loop(0, n_t, table_step, 0)
+
+    gain1 = gain1_ref[...]
+    gain2 = gain2_ref[...]
+
+    def norm_step(i, c):
+        j = lax.rem(t + i, n_t)
+
+        @pl.when(i > 0)
+        def _():
+            t_got(0, xg, j)
+
+        unit, _ = rms_parts(xg[j].astype(F32))
+        n1[j] = (unit * gain1).astype(BF)
+        return c
+
+    lax.fori_loop(0, n_t, norm_step, 0)
+
+    for o in range(1, n_dp):
+        p = lax.rem(d + o, n_dp)
+        d_got(0, ag.at[wslice(p)], p)
+    wo[...] = ag[:, qkv_cols:]
+
+    def qkv_step(j, c):
+        mixed = dot(n1[j], ag[:, :qkv_cols])
+        cosine = cosb[j]
+        sine = sinb[j]
+        for k in range(2 * n_head // 2):
+            chunk = mixed[:, 128 * k:128 * k + 128]
+            chunk = chunk * cosine + partner(chunk) * sine
+            for half in range(2):
+                idx = 2 * k + half
+                part = chunk[:, 64 * half:64 * half + 64]
+                if idx < n_head:
+                    part = part.astype(BF).astype(F32) * 0.125
+                qkvh[idx, j] = part.astype(BF)
+        for h in range(n_head):
+            lo = 2 * head_cols + HD * h
+            qkvh[2 * n_head + h, j] = mixed[:, lo:lo + HD].astype(BF)
+        return c
+
+    lax.fori_loop(0, n_t, qkv_step, 0)
+
+    def attn_step(i, c):
+        h = i // n_t
+        j = lax.rem(i, n_t)
+        keys = qkvh[n_head + h].reshape(span, HD)
+        vals = qkvh[2 * n_head + h].reshape(span, HD)
+        s = dot(qkvh[h, j], keys, LAST) + bias[j]
+        e = jnp.exp(s - jnp.max(s, axis=-1, keepdims=True))
+        p = e * (1.0 / jnp.sum(e, axis=-1, keepdims=True))
+        probs[h, j] = p
+        hoh[h, j] = dot(p.astype(BF), vals).astype(BF)
+        return c
+
+    lax.fori_loop(0, n_head * n_t, attn_step, 0)
+
+    def send_part(stage, part, j, own, snd, rcv):
+        @pl.when(j == t)
+        def _():
+            own[...] = part
+
+        @pl.when(j != t)
+        def _():
+            snd[j] = part.astype(BF)
+            t_copy(stage, snd.at[j], rcv.at[t], j, t).start()
+
+    def order(i):
+        return lax.rem(t + (2 + i) * (1 - i // 2) + (3 - i) * (i // 2), n_t)
+
+    def attn_out_step(i, c):
+        j = order(i)
+        flat = jnp.concatenate([hoh[h, j] for h in range(n_head)], axis=1)
+        hof[j] = flat
+        send_part(2, dot(flat, wo[...], LAST), j, own1, rs1s, rs1r)
+        return c
+
+    lax.fori_loop(0, n_t, attn_out_step, 0)
+
+    def collect(stage, own, rcv):
+        total = own[...]
+        for o in range(1, n_t):
+            p = lax.rem(t + o, n_t)
+            t_got(stage, rcv, p)
+            total = total + rcv[p].astype(F32)
+        return total
+
+    for o in range(1, n_dp):
+        p = lax.rem(d + o, n_dp)
+        d_got(1, bg.at[wslice(p)], p)
+    wg[...] = bg[:, :ff]
+    wu[...] = bg[:, ff:2 * ff]
+    wd[...] = bg[:, 2 * ff:3 * ff]
+
+    def hidden_step(i, c):
+        j = lax.rem(t + i, n_t)
+
+        @pl.when(i > 0)
+        def _():
+            t_got(1, cg, j)
+
+        ghf[j] = dot(cg[j], wd[...])
+        return c
+
+    lax.fori_loop(0, n_t, hidden_step, 0)
+
+    resid_mid = x_ref[...].astype(F32) + collect(2, own1, rs1r)
+    mid[...] = resid_mid
+    unit, inv2 = rms_parts(resid_mid)
+    unit2[...] = unit
+    n2g[t] = (unit * gain2).astype(BF)
+    t_spread(3, n2g.at[t], n2g)
+
+    def ffn_step(i, c):
+        j = lax.rem(t + i, n_t)
+
+        @pl.when(i > 0)
+        def _():
+            t_got(3, n2g, j)
+
+        gate = dot(n2g[j], wg[...])
+        up = dot(n2g[j], wu[...])
+        cdf = 0.5 * (1.0 + lax.erf(gate * 0.7071067811865476))
+        density = 0.3989422804014327 * jnp.exp(-0.5 * gate * gate)
+        val = gate * cdf
+        slope = cdf + gate * density
+        hidden = (val * up).astype(BF)
+        grad_hidden = ghf[j]
+        m0 = (grad_hidden * up * slope).astype(BF)
+        m1 = (grad_hidden * val).astype(BF)
+        hid[j] = hidden
+        mix0[j] = m0
+        mix1[j] = m1
+        send_part(4, dot(m0, wg[...], LAST) + dot(m1, wu[...], LAST), j, own2, rs2s, rs2r)
+        send_part(5, dot(hidden, wd[...], LAST), j, own3, rs3s, rs3r)
+        return c
+
+    lax.fori_loop(0, n_t, ffn_step, 0)
+
+    grad_two = collect(4, own2, rs2r)
+    unit = unit2[...]
+    gain_ffn_part = jnp.sum(grad_two * unit, axis=0, keepdims=True)
+    grad_mid = cot_ref[...].astype(F32) + norm_back(grad_two, unit, inv2, gain2)
+    gmid[...] = grad_mid
+    gmg[t] = grad_mid.astype(BF)
+    t_spread(6, gmg.at[t], gmg)
+
+    def flat_cols(buf, lo, n):
+        return buf[:, :, lo:lo + n].reshape(span, n)
+
+    tile = 256
+    hid_all = hid[...].reshape(span, ff)
+    mix0_all = mix0[...].reshape(span, ff)
+    mix1_all = mix1[...].reshape(span, ff)
+    for lo in range(0, width, tile):
+        lhs = flat_cols(n2g, lo, tile)
+        bgs[lo:lo + tile, :ff] = dot(lhs, mix0_all, FIRST).astype(BF)
+        bgs[lo:lo + tile, ff:2 * ff] = dot(lhs, mix1_all, FIRST).astype(BF)
+        bgs[lo:lo + tile, 2 * ff:3 * ff] = dot(flat_cols(cg, lo, tile), hid_all, FIRST).astype(BF)
+    bgs[:, 3 * ff:] = jnp.zeros((width, bgs.shape[1] - 3 * ff), BF)
+    for o in range(1, n_dp):
+        p = lax.rem(d + o, n_dp)
+        d_copy(2, bgs.at[wslice(p)], bgr.at[d], p, d).start()
+
+    def grad_heads_step(i, c):
+        j = lax.rem(t + i, n_t)
+
+        @pl.when(i > 0)
+        def _():
+            t_got(6, gmg, j)
+
+        gh = dot(gmg[j], wo[...]).astype(BF)
+        for h in range(n_head):
+            ghh[h, j] = gh[:, HD * h:HD * h + HD]
+        return c
+
+    lax.fori_loop(0, n_t, grad_heads_step, 0)
+
+    def attn_back(h, c):
+        keys = qkvh[n_head + h].reshape(span, HD)
+        vals = qkvh[2 * n_head + h].reshape(span, HD)
+
+        def step(j, c2):
+            gh = ghh[h, j]
+            row_dot = jnp.sum(gh.astype(F32) * hoh[h, j].astype(F32), axis=-1, keepdims=True)
+            ds = (probs[h, j] * (dot(gh, vals, LAST) - row_dot)).astype(BF)
+            dsb[j] = ds
+            dqkv[h, j] = dot(ds, keys) * 0.125
+            return c2
+
+        lax.fori_loop(0, n_t, step, 0)
+        dk = dot(dsb[...].reshape(span, span), qkvh[h].reshape(span, HD), FIRST)
+        dqkv[n_head + h] = dk.reshape(n_t, rows, HD)
+        pb = probs[h].reshape(span, span).astype(BF)
+        dv = dot(pb, ghh[h].reshape(span, HD), FIRST)
+        dqkv[2 * n_head + h] = dv.reshape(n_t, rows, HD)
+        return c
+
+    lax.fori_loop(0, n_head, attn_back, 0)
+
+    def qkv_back_step(i, c):
+        j = order(i)
+        cosine = cosb[j]
+        sine = sinb[j]
+        parts = []
+        for k in range(n_head):
+            chunk = jnp.concatenate([dqkv[2 * k, j], dqkv[2 * k + 1, j]], axis=1)
+            parts.append(chunk * cosine - partner(chunk) * sine)
+        parts = parts + [dqkv[2 * n_head + h, j] for h in range(n_head)]
+        grads = jnp.concatenate(parts, axis=1).astype(BF)
+        gq[j] = grads
+        send_part(7, dot(grads, ag[:, :qkv_cols], LAST), j, own4, rs4s, rs4r)
+        return c
+
+    lax.fori_loop(0, n_t, qkv_back_step, 0)
+
+    gq_all = gq[...].reshape(span, qkv_cols)
+    ho_all = hof[...].reshape(span, head_cols)
+    for lo in range(0, width, tile):
+        ags[lo:lo + tile, :qkv_cols] = dot(flat_cols(n1, lo, tile), gq_all, FIRST).astype(BF)
+        ags[lo:lo + tile, qkv_cols:] = dot(flat_cols(gmg, lo, tile), ho_all, FIRST).astype(BF)
+    for o in range(1, n_dp):
+        p = lax.rem(d + o, n_dp)
+        d_copy(3, ags.at[wslice(p)], agr.at[d], p, d).start()
+
+    grad_one = collect(7, own4, rs4r)
+    unit1, inv1 = rms_parts(x_ref[...].astype(F32))
+    gain_attn_part = jnp.sum(grad_one * unit1, axis=0, keepdims=True)
+    gpt[t] = jnp.concatenate([gain_attn_part, gain_ffn_part, jnp.zeros((6, width), F32)], axis=0)
+    t_spread(8, gpt.at[t], gpt)
+    gin_ref[...] = gmid[...] + norm_back(grad_one, unit1, inv1, gain1)
+    out_ref[...] = (mid[...] + collect(5, own3, rs3r)).astype(BF)
+
+    for o in range(1, n_t):
+        t_got(8, gpt, lax.rem(t + o, n_t))
+    gpd[d] = jnp.sum(gpt[...], axis=0)
+    for o in range(1, n_dp):
+        d_copy(4, gpd.at[d], gpd.at[d], lax.rem(d + o, n_dp), d).start()
+
+    total = bgs[wslice(d), :].astype(F32)
+    for o in range(1, n_dp):
+        p = lax.rem(d + o, n_dp)
+        d_got(2, bgr.at[p], p)
+        total = total + bgr[p].astype(F32)
+    gb_ref[...] = total
+
+    total = ags[wslice(d), :].astype(F32)
+    for o in range(1, n_dp):
+        p = lax.rem(d + o, n_dp)
+        d_got(3, agr.at[p], p)
+        total = total + agr[p].astype(F32)
+    ga_ref[...] = total
+
+    for o in range(1, n_dp):
+        p = lax.rem(d + o, n_dp)
+        d_got(4, gpd.at[p], p)
+    gains_ref[...] = jnp.sum(gpd[...], axis=0)
+
+    for o in range(1, n_t):
+        p = lax.rem(t + o, n_t)
+        for stage, ref in enumerate((xg, cg, rs1s, n2g, rs2s, rs3s, gmg, rs4s, gpt)):
+            t_copy(stage, ref.at[p], ref.at[p], p, p).wait_send()
+    for o in range(1, n_dp):
+        p = lax.rem(d + o, n_dp)
+        for stage, ref in enumerate((a_ref, b_ref, bgr.at[p], agr.at[p], gpd.at[p])):
+            d_copy(stage, ref, ref, p, p).wait_send()
+
+
+def on_device_fused(
+    n_dp, n_t,
+    inputs, segment_ids, gain_attn, gain_ffn, query_key_value_weight, w_out, w_ffn_in, w_ffn_out, cotangent,
+):
+    rows, width = inputs.shape
+    wrows = w_out.shape[0]
+    head_cols = w_out.shape[1]
+    ff = w_ffn_out.shape[1]
+    if n_t != 4 or wrows % 16 or rows % 128 or head_cols % HD:
+        return on_device(
+            inputs, segment_ids, gain_attn, gain_ffn, query_key_value_weight, w_out, w_ffn_in, w_ffn_out, cotangent
+        )
+    n_head = head_cols // HD
+    span = n_t * rows
+    a_cols = 4 * head_cols
+    b_cols = -(-3 * ff // 128) * 128
+    block_a = jnp.concatenate([query_key_value_weight.reshape(wrows, -1), w_out], axis=1)
+    block_b = jnp.concatenate(
+        [w_ffn_in.reshape(wrows, -1), w_ffn_out, jnp.zeros((wrows, b_cols - 3 * ff), BF)], axis=1
+    )
+    half = np.arange(32, dtype=np.float64)
+    freq = np.tile(THETA ** (-2.0 * half / HD), 4).astype(np.float32)[None]
+    vmem = pl.BlockSpec(memory_space=pltpu.VMEM)
+    act = (n_t, rows, width)
+
+    def v(shape, kind=BF):
+        return pltpu.VMEM(shape, kind)
+
+    scratch = [
+        v(act), v(act), v((width, a_cols)), v((width, b_cols)), v(act), v(act), v(act),
+        v((n_t, rows, 128), F32), v((n_t, rows, 128), F32), v((n_t, rows, span), F32),
+        v((3 * n_head, n_t, rows, HD)), v((n_head, n_t, rows, span), F32), v((n_head, n_t, rows, HD)),
+        v((n_t, rows, head_cols)), v((width, head_cols)), v((width, ff)), v((width, ff)), v((width, ff)),
+        v(act), v(act), v(act), v(act), v(act), v(act), v(act), v(act),
+        v((rows, width), F32), v((rows, width), F32), v((rows, width), F32), v((rows, width), F32),
+        v((n_t, rows, ff), F32), v((n_t, rows, ff)), v((n_t, rows, ff)), v((n_t, rows, ff)),
+        v((rows, width), F32), v((rows, width), F32), v((rows, width), F32),
+        v((n_head, n_t, rows, HD)), v((n_t, rows, span)), v((3 * n_head, n_t, rows, HD), F32),
+        v((n_t, rows, 3 * head_cols)),
+        v((width, a_cols)), v((n_dp, wrows, a_cols)), v((width, b_cols)), v((n_dp, wrows, b_cols)),
+        v((n_t, 8, width), F32), v((n_dp, 8, width), F32),
+        pltpu.SemaphoreType.DMA((9, n_t)), pltpu.SemaphoreType.DMA((9, n_t)),
+        pltpu.SemaphoreType.DMA((5, n_dp)), pltpu.SemaphoreType.DMA((5, n_dp)),
+    ]
+    result, grad_input, gains, grad_a, grad_b = pl.pallas_call(
+        functools.partial(fused_kernel, n_dp, n_t, n_head, ff),
+        out_shape=(
+            jax.ShapeDtypeStruct((rows, width), BF),
+            jax.ShapeDtypeStruct((rows, width), F32),
+            jax.ShapeDtypeStruct((8, width), F32),
+            jax.ShapeDtypeStruct((wrows, a_cols), F32),
+            jax.ShapeDtypeStruct((wrows, b_cols), F32),
+        ),
+        in_specs=[vmem] * 8,
+        out_specs=(vmem,) * 5,
+        scratch_shapes=scratch,
+        compiler_params=pltpu.CompilerParams(
+            collective_id=0, has_side_effects=True, vmem_limit_bytes=60 * 1024 * 1024
+        ),
+        name="fused_layer",
+    )(
+        inputs, cotangent, segment_ids, gain_attn[None], gain_ffn[None], jnp.asarray(freq), block_a, block_b,
+    )
+    return (
+        result,
+        grad_input,
+        gains[0],
+        gains[1],
+        grad_a[:, : 3 * head_cols].reshape(wrows, 3, head_cols),
+        grad_a[:, 3 * head_cols:],
+        grad_b[:, : 2 * ff].reshape(wrows, 2, ff),
+        grad_b[:, 2 * ff:3 * ff],
+    )
+
+
 def solution(mesh):
     return jax.shard_map(
-        on_device,
+        functools.partial(on_device_fused, mesh.shape["dp"], mesh.shape["tensor"]),
         mesh=mesh,
         in_specs=(
             P(("dp", "tensor"), None),

time: 563 us -> 158 us (0.28)
  waiting for transfers between devices: 292 us -> 0 us
  blocking collectives: 206 us -> 0 us
  Pallas kernels: 0 us -> 143 us
  matrix products: 22.8 us -> 0 us
  between operations: 14.8 us -> 0.72 us
  other arithmetic: 13.8 us -> 1.51 us
    reduce_scatter x7 -> x0, waiting for transfers between devices: 268 us -> none  [the longest x1 72.3 us: on_device(): lax.psum_scatter(gradient_query_key_value, 'dp', scatter_dimension=0, til...]
    all_gather x8 -> x0, blocking collectives: 167 us -> none  [the longest x2 34.8 us: spread_grads(): return lax.all_gather(row_data, 'tensor', axis=0, tiled=True)]
    pallas_call x0 -> x1, Pallas kernels: none -> 143 us  [on_device_fused(): pl.pallas_call(functools.partial(fused_kernel, n_dp, n_t, n_head, ff), ou...]
    psum x1 -> x0, blocking collectives: 38.5 us -> none  [on_device(): lax.psum((gain_attn_part, gain_ffn_part), ('dp', 'tensor'))]
    unnamed x9 -> x0, waiting for transfers between devices: 23.6 us -> none
    dot_general x17 -> x0, matrix products: 22.1 us -> none  [the longest x1 3.02 us: on_device(): lax.dot_general(hidden, full_down, contract_last, preferred_element_type=...]
    reduce_sum x8 -> x0, other arithmetic: 6.7 us -> none  [the longest x2 2.15 us: normalize(): centre = row_data - jnp.mean(row_data, axis=-1, keepdims=True)]
  transfers between devices with their start and end apart: 8 -> 0, of which waited for: 7 -> 0; matrix products, arithmetic and copies ran while one was open for 4% -> 0% of each run, Pallas kernels for 0% -> 0%
where the time goes in v1:
time: 158 us
  Pallas kernels  143 us (91%)
  local copies, waits for them, and re-layouts  12.4 us (8%)
    pallas_call x1, Pallas kernels, on_device_fused(): pl.pallas_call(functools.partial(fused_kernel, n_dp, n_t, n_head, ff), ou...  143 us
    unnamed x20, local copies, waits for them, and re-layouts  4.06 us

profile of v1, /device:TPU:25, one launch (start us, length us, event | category | flops | bytes accessed | tf_op | source)
XLA Modules:
  0.0 157.8 jit_solution(2260535210519845120)
XLA Ops:
  0.6 0.0 copy-start.6
  0.7 0.1 pad.2.clone
  0.7 0.6 copy-done.6
  1.3 0.0 copy-start.7
  1.3 0.6 broadcast_in_dim.9.gain1_ref
  1.9 0.1 copy-done.7
  2.0 0.6 broadcast_in_dim.10.gain2_ref
  2.6 0.0 copy-start.4
  2.6 1.1 reshape.29
  3.7 0.0 copy-done.4
  3.7 0.0 copy-start.3
  3.7 0.8 maximum_maximum_fusion.b_ref
  4.5 0.1 copy-done.3
  4.6 0.2 copy.20
  4.8 0.1 copy.21
  4.9 0.6 copy-done.5
  5.6 0.7 pad_maximum_fusion.a_ref
  6.3 143.2 %fused_layer.1 = (bf16[128,768]{1,0:T(8,128)(2,1)}, f32[128,768]{1,0:T(8,128)}, f32[8,768]{1,0:T(8,128)}, f32[96,768]{1,0:T(8,128)}, f32[96,896]{1,0:T(8,128)}) custom-call(bf16[128,768]{1,0:T(8,128)(2,1)} %x_ref.1, bf16[128,768]{1,0:T(8,128)(2,1)} %cot_ref.1, s32[1,512]{1,0:T(1,128)} %seg_ref.1, f32[1,768]{1,0:T(1,128)} %broadcast_in_dim.9.gain1_ref, ...), custom_call_target="tpu_custom_call" | custom-call | tf_op jit(solution)/shard_map/fused_layer/pallas_call | solution.py:654
  149.5 1.4 slice_reduce_fusion
  150.9 1.6 %slice.21 = f32[96,192]{1,0:T(8,128)} slice(f32[96,768]{1,0:T(8,128)} %get-tuple-element.16), slice={[0:96], [576:768]} | slice | bytes 147456 | tf_op jit(solution)/shard_map/slice | solution.py:679
  152.6 1.0 slice.20
  153.5 0.1 copy.22
  153.7 0.0 copy-start
  153.7 0.9 copy.23
  154.6 0.1 copy-done
  154.7 0.8 slice.23
  155.4 0.0 copy-start.1
  155.5 0.9 reshape.31
  156.4 0.0 copy-done.2
  156.4 0.7 copy.26
  157.1 0.0 copy-done.1
  157.1 0.7 copy.27
  (4 shorter events, 0.0 us)
Async XLA Ops:
  0.6 0.7 copy-start.6
  1.3 0.7 copy-start.7
  2.6 1.1 copy-start.4
  3.7 0.9 copy-start.3
  4.8 0.8 copy-start.5
  153.7 1.0 copy-start
  155.4 1.0 copy-start.2
  155.4 1.6 %copy-start.1 = (f32[128,768]{1,0:T(8,128)S(1)}, f32[128,768]{1,0:T(8,128)}, u32[]{:S(2)}) copy-start(f32[128,768]{1,0:T(8,128)} %get-tuple-element.45) | copy-start | bytes 1179652

commit v2 on v1

--- a/solution.py
+++ b/solution.py
@@ -269,7 +269,7 @@
     out_ref, gin_ref, gains_ref, ga_ref, gb_ref,
     xg, cg, ag, bg, n1, n2g, gmg, cosb, sinb, bias, qkvh, probs, hoh, hof, wo, wg, wu, wd,
     rs1s, rs1r, rs2s, rs2r, rs3s, rs3r, rs4s, rs4r, own1, own2, own3, own4,
-    ghf, hid, mix0, mix1, unit2, mid, gmid, ghh, dsb, dqkv, gq, ags, agr, bgs, bgr, gpt, gpd,
+    ghf, hid, mix0, mix1, unit2, mid, gmid, ghh, dsb, dqkv, gq, ags, axr, azs, azr, bgs, bxr, bzs, bzr, gpt, gpd,
     t_send, t_recv, d_send, d_recv,
 ):
     d = lax.axis_index("dp")
@@ -292,9 +292,16 @@
             src_ref=src, dst_ref=dst, send_sem=t_send.at[stage, to], recv_sem=t_recv.at[stage, slot],
             device_id=(d, to), device_id_type=pl.DeviceIdType.MESH)
 
-    def d_copy(stage, src, dst, to, slot):
+    xx = lax.rem(d, 2)
+    zz = d // 2
+    n_z = n_dp // 2
+    across = d + 1 - 2 * xx
+    z_peers = [lax.rem(zz + o, n_z) for o in range(1, n_z)]
+
+    def d_copy(stage, src, dst, to, slot, lane=None, at=None):
+        send = d_send.at[stage if lane is None else lane, to if at is None else at]
         return pltpu.make_async_remote_copy(
-            src_ref=src, dst_ref=dst, send_sem=d_send.at[stage, to], recv_sem=d_recv.at[stage, slot],
+            src_ref=src, dst_ref=dst, send_sem=send, recv_sem=d_recv.at[stage, slot],
             device_id=(to, t), device_id_type=pl.DeviceIdType.MESH)
 
     def t_spread(stage, src, buf):
@@ -311,11 +318,12 @@
         return pl.ds(pl.multiple_of(p * wrows, 16), wrows)
 
     t_spread(0, x_ref, xg)
-    for o in range(1, n_dp):
-        d_copy(0, a_ref, ag.at[wslice(d)], lax.rem(d + o, n_dp), d).start()
+    for z in z_peers:
+        d_copy(0, a_ref, ag.at[wslice(d)], 2 * z + xx, d).start()
+    d_copy(0, a_ref, ag.at[wslice(d)], across, d).start()
     t_spread(1, cot_ref, cg)
-    for o in range(1, n_dp):
-        d_copy(1, b_ref, bg.at[wslice(d)], lax.rem(d + o, n_dp), d).start()
+    for z in z_peers:
+        d_copy(1, b_ref, bg.at[wslice(d)], 2 * z + xx, d).start()
     xg[t] = x_ref[...]
     cg[t] = cot_ref[...]
     ag[wslice(d), :] = a_ref[...]
@@ -357,9 +365,20 @@
 
     lax.fori_loop(0, n_t, norm_step, 0)
 
-    for o in range(1, n_dp):
-        p = lax.rem(d + o, n_dp)
-        d_got(0, ag.at[wslice(p)], p)
+    def pass_on(stage, buf, z):
+        p = 2 * z + xx
+        d_got(stage, buf.at[wslice(p)], p)
+        d_copy(stage, buf.at[wslice(p)], buf.at[wslice(p)], across, p, 5 + stage, p).start()
+
+    def from_across(stage, buf):
+        for z in range(n_z):
+            p = 2 * z + 1 - xx
+            d_got(stage, buf.at[wslice(p)], p)
+
+    for z in z_peers:
+        pass_on(0, ag, z)
+    d_copy(1, b_ref, bg.at[wslice(d)], across, d).start()
+    from_across(0, ag)
     wo[...] = ag[:, qkv_cols:]
 
     def qkv_step(j, c):
@@ -382,9 +401,7 @@
 
     lax.fori_loop(0, n_t, qkv_step, 0)
 
-    def attn_step(i, c):
-        h = i // n_t
-        j = lax.rem(i, n_t)
+    def attn_step(h, j, c):
         keys = qkvh[n_head + h].reshape(span, HD)
         vals = qkvh[2 * n_head + h].reshape(span, HD)
         s = dot(qkvh[h, j], keys, LAST) + bias[j]
@@ -394,7 +411,13 @@
         hoh[h, j] = dot(p.astype(BF), vals).astype(BF)
         return c
 
-    lax.fori_loop(0, n_head * n_t, attn_step, 0)
+    passed = 0
+    for h in range(n_head):
+        lax.fori_loop(0, n_t, functools.partial(attn_step, h), 0)
+        until = n_z - 1 if h == n_head - 1 else min(passed + 1, n_z - 1)
+        for z in z_peers[passed:until]:
+            pass_on(1, bg, z)
+        passed = until
 
     def send_part(stage, part, j, own, snd, rcv):
         @pl.when(j == t)
@@ -426,9 +449,7 @@
             total = total + rcv[p].astype(F32)
         return total
 
-    for o in range(1, n_dp):
-        p = lax.rem(d + o, n_dp)
-        d_got(1, bg.at[wslice(p)], p)
+    from_across(1, bg)
     wg[...] = bg[:, :ff]
     wu[...] = bg[:, ff:2 * ff]
     wd[...] = bg[:, 2 * ff:3 * ff]
@@ -499,9 +520,26 @@
         bgs[lo:lo + tile, ff:2 * ff] = dot(lhs, mix1_all, FIRST).astype(BF)
         bgs[lo:lo + tile, 2 * ff:3 * ff] = dot(flat_cols(cg, lo, tile), hid_all, FIRST).astype(BF)
     bgs[:, 3 * ff:] = jnp.zeros((width, bgs.shape[1] - 3 * ff), BF)
-    for o in range(1, n_dp):
-        p = lax.rem(d + o, n_dp)
-        d_copy(2, bgs.at[wslice(p)], bgr.at[d], p, d).start()
+
+    def reduce_across(stage, snd, rcv):
+        for z in range(n_z):
+            d_copy(stage, snd.at[wslice(2 * z + 1 - xx)], rcv.at[z], across, z, stage, z).start()
+
+    def reduce_along(stage, snd, rcv, sums, got):
+        for z in z_peers:
+            d_got(stage, rcv.at[z], z)
+            sums[z] = (snd[wslice(2 * z + xx), :].astype(F32) + rcv[z].astype(F32)).astype(BF)
+            d_copy(stage + 5, sums.at[z], got.at[zz], 2 * z + xx, zz, stage + 5, z).start()
+
+    def reduce_end(stage, snd, rcv, got):
+        d_got(stage, rcv.at[zz], zz)
+        total = snd[wslice(d), :].astype(F32) + rcv[zz].astype(F32)
+        for z in z_peers:
+            d_got(stage + 5, got.at[z], z)
+            total = total + got[z].astype(F32)
+        return total
+
+    reduce_across(2, bgs, bxr)
 
     def grad_heads_step(i, c):
         j = lax.rem(t + i, n_t)
@@ -539,8 +577,9 @@
 
     lax.fori_loop(0, n_head, attn_back, 0)
 
-    def qkv_back_step(i, c):
-        j = order(i)
+    reduce_along(2, bgs, bxr, bzs, bzr)
+
+    def unrotate_step(j, c):
         cosine = cosb[j]
         sine = sinb[j]
         parts = []
@@ -548,21 +587,25 @@
             chunk = jnp.concatenate([dqkv[2 * k, j], dqkv[2 * k + 1, j]], axis=1)
             parts.append(chunk * cosine - partner(chunk) * sine)
         parts = parts + [dqkv[2 * n_head + h, j] for h in range(n_head)]
-        grads = jnp.concatenate(parts, axis=1).astype(BF)
-        gq[j] = grads
-        send_part(7, dot(grads, ag[:, :qkv_cols], LAST), j, own4, rs4s, rs4r)
-        return c
-
-    lax.fori_loop(0, n_t, qkv_back_step, 0)
+        gq[j] = jnp.concatenate(parts, axis=1).astype(BF)
+        return c
+
+    lax.fori_loop(0, n_t, unrotate_step, 0)
 
     gq_all = gq[...].reshape(span, qkv_cols)
     ho_all = hof[...].reshape(span, head_cols)
     for lo in range(0, width, tile):
         ags[lo:lo + tile, :qkv_cols] = dot(flat_cols(n1, lo, tile), gq_all, FIRST).astype(BF)
         ags[lo:lo + tile, qkv_cols:] = dot(flat_cols(gmg, lo, tile), ho_all, FIRST).astype(BF)
-    for o in range(1, n_dp):
-        p = lax.rem(d + o, n_dp)
-        d_copy(3, ags.at[wslice(p)], agr.at[d], p, d).start()
+    reduce_across(3, ags, axr)
+
+    def qkv_back_step(i, c):
+        j = order(i)
+        send_part(7, dot(gq[j], ag[:, :qkv_cols], LAST), j, own4, rs4s, rs4r)
+        return c
+
+    lax.fori_loop(0, n_t, qkv_back_step, 0)
+    reduce_along(3, ags, axr, azs, azr)
 
     grad_one = collect(7, own4, rs4r)
     unit1, inv1 = rms_parts(x_ref[...].astype(F32))
@@ -578,19 +621,8 @@
     for o in range(1, n_dp):
         d_copy(4, gpd.at[d], gpd.at[d], lax.rem(d + o, n_dp), d).start()
 
-    total = bgs[wslice(d), :].astype(F32)
-    for o in range(1, n_dp):
-        p = lax.rem(d + o, n_dp)
-        d_got(2, bgr.at[p], p)
-        total = total + bgr[p].astype(F32)
-    gb_ref[...] = total
-
-    total = ags[wslice(d), :].astype(F32)
-    for o in range(1, n_dp):
-        p = lax.rem(d + o, n_dp)
-        d_got(3, agr.at[p], p)
-        total = total + agr[p].astype(F32)
-    ga_ref[...] = total
+    gb_ref[...] = reduce_end(2, bgs, bxr, bzr)
+    ga_ref[...] = reduce_end(3, ags, axr, azr)
 
     for o in range(1, n_dp):
         p = lax.rem(d + o, n_dp)
@@ -601,10 +633,20 @@
         p = lax.rem(t + o, n_t)
         for stage, ref in enumerate((xg, cg, rs1s, n2g, rs2s, rs3s, gmg, rs4s, gpt)):
             t_copy(stage, ref.at[p], ref.at[p], p, p).wait_send()
+
+    def d_sent(lane, ref, at):
+        d_copy(0, ref, ref, across, d, lane, at).wait_send()
+
     for o in range(1, n_dp):
-        p = lax.rem(d + o, n_dp)
-        for stage, ref in enumerate((a_ref, b_ref, bgr.at[p], agr.at[p], gpd.at[p])):
-            d_copy(stage, ref, ref, p, p).wait_send()
+        d_sent(4, gpd.at[d], lax.rem(d + o, n_dp))
+    for lane, own, part, sums in ((0, a_ref, axr, azs), (1, b_ref, bxr, bzs)):
+        d_sent(lane, own, across)
+        for z in z_peers:
+            d_sent(lane, own, 2 * z + xx)
+            d_sent(lane + 5, own, 2 * z + xx)
+            d_sent(8 - lane, sums.at[z], z)
+        for z in range(n_z):
+            d_sent(3 - lane, part.at[z], z)
 
 
 def on_device_fused(
@@ -615,7 +657,7 @@
     wrows = w_out.shape[0]
     head_cols = w_out.shape[1]
     ff = w_ffn_out.shape[1]
-    if n_t != 4 or wrows % 16 or rows % 128 or head_cols % HD:
+    if n_t != 4 or n_dp % 2 or wrows % 16 or rows % 128 or head_cols % HD:
         return on_device(
             inputs, segment_ids, gain_attn, gain_ffn, query_key_value_weight, w_out, w_ffn_in, w_ffn_out, cotangent
         )
@@ -631,6 +673,9 @@
     freq = np.tile(THETA ** (-2.0 * half / HD), 4).astype(np.float32)[None]
     vmem = pl.BlockSpec(memory_space=pltpu.VMEM)
     act = (n_t, rows, width)
+
+    part_a = (n_dp // 2, wrows, a_cols)
+    part_b = (n_dp // 2, wrows, b_cols)
 
     def v(shape, kind=BF):
         return pltpu.VMEM(shape, kind)
@@ -646,10 +691,10 @@
         v((rows, width), F32), v((rows, width), F32), v((rows, width), F32),
         v((n_head, n_t, rows, HD)), v((n_t, rows, span)), v((3 * n_head, n_t, rows, HD), F32),
         v((n_t, rows, 3 * head_cols)),
-        v((width, a_cols)), v((n_dp, wrows, a_cols)), v((width, b_cols)), v((n_dp, wrows, b_cols)),
+        v((width, a_cols)), v(part_a), v(part_a), v(part_a), v((width, b_cols)), v(part_b), v(part_b), v(part_b),
         v((n_t, 8, width), F32), v((n_dp, 8, width), F32),
         pltpu.SemaphoreType.DMA((9, n_t)), pltpu.SemaphoreType.DMA((9, n_t)),
-        pltpu.SemaphoreType.DMA((5, n_dp)), pltpu.SemaphoreType.DMA((5, n_dp)),
+        pltpu.SemaphoreType.DMA((9, n_dp)), pltpu.SemaphoreType.DMA((9, n_dp)),
     ]
     result, grad_input, gains, grad_a, grad_b = pl.pallas_call(
         functools.partial(fused_kernel, n_dp, n_t, n_head, ff),

time: 158 us -> 141 us (0.89)
  Pallas kernels: 143 us -> 126 us
    pallas_call x1, Pallas kernels: 143 us -> 126 us  [on_device_fused(): pl.pallas_call(functools.partial(fused_kernel, n_dp, n_t, n_head, ff), ou...]
where the time goes in v2:
time: 141 us; the launch traced here: 140 us
  Pallas kernels  126 us (89%)
  local copies, waits for them, and re-layouts  12.4 us (9%)
  other arithmetic  1.51 us (1%)
    pallas_call x1, Pallas kernels, on_device_fused(): pl.pallas_call(functools.partial(fused_kernel, n_dp, n_t, n_head, ff), ou...  126 us
    unnamed x20, local copies, waits for them, and re-layouts  4.06 us

profile of v2, /device:TPU:25, one launch (start us, length us, event | category | flops | bytes accessed | tf_op | source)
XLA Modules:
  0.0 140.5 jit_solution(12571616260815321742)
XLA Ops:
  0.6 0.0 copy-start.6
  0.7 0.1 pad.2.clone
  0.7 0.6 copy-done.6
  1.3 0.0 copy-start.7
  1.3 0.6 broadcast_in_dim.9.gain1_ref
  1.9 0.1 copy-done.7
  2.0 0.6 broadcast_in_dim.10.gain2_ref
  2.6 0.0 copy-start.4
  2.6 1.1 reshape.29
  3.7 0.0 copy-done.4
  3.7 0.0 copy-start.3
  3.7 0.8 maximum_maximum_fusion.b_ref
  4.5 0.1 copy-done.3
  4.6 0.2 copy.20
  4.8 0.1 copy.21
  4.9 0.6 copy-done.5
  5.6 0.7 pad_maximum_fusion.a_ref
  6.3 125.8 %fused_layer.1 = (bf16[128,768]{1,0:T(8,128)(2,1)}, f32[128,768]{1,0:T(8,128)}, f32[8,768]{1,0:T(8,128)}, f32[96,768]{1,0:T(8,128)}, f32[96,896]{1,0:T(8,128)}) custom-call(bf16[128,768]{1,0:T(8,128)(2,1)} %x_ref.1, bf16[128,768]{1,0:T(8,128)(2,1)} %cot_ref.1, s32[1,512]{1,0:T(1,128)} %seg_ref.1, f32[1,768]{1,0:T(1,128)} %broadcast_in_dim.9.gain1_ref, ...), custom_call_target="tpu_custom_call" | custom-call | tf_op jit(solution)/shard_map/fused_layer/pallas_call | solution.py:699
  132.2 1.4 %slice_reduce_fusion = (f32[768]{0:T(1024)}, f32[768]{0:T(1024)}) fusion(f32[8,768]{1,0:T(8,128)} %get-tuple-element.15), kind=kLoop, calls=%fused_computation.2 | loop fusion | bytes 12288 | tf_op jit(solution)/shard_map/slice | solution.py:722
  133.6 1.6 %slice.21 = f32[96,192]{1,0:T(8,128)} slice(f32[96,768]{1,0:T(8,128)} %get-tuple-element.16), slice={[0:96], [576:768]} | slice | bytes 147456 | tf_op jit(solution)/shard_map/slice | solution.py:724
  135.2 1.0 slice.20
  136.2 0.1 copy.22
  136.3 0.0 copy-start
  136.3 0.9 copy.23
  137.2 0.1 copy-done
  137.3 0.8 slice.23
  138.1 0.0 copy-start.1
  138.1 0.9 reshape.31
  139.1 0.0 copy-done.2
  139.1 0.7 copy.26
  139.7 0.0 copy-done.1
  139.7 0.7 copy.27
  (4 shorter events, 0.0 us)
Async XLA Ops:
  0.6 0.7 copy-start.6
  1.3 0.7 copy-start.7
  2.6 1.1 copy-start.4
  3.7 0.9 copy-start.3
  4.8 0.8 copy-start.5
  136.3 1.0 copy-start
  138.1 1.0 copy-start.2
  138.1 1.6 %copy-start.1 = (f32[128,768]{1,0:T(8,128)S(1)}, f32[128,768]{1,0:T(8,128)}, u32[]{:S(2)}) copy-start(f32[128,768]{1,0:T(8,128)} %get-tuple-element.45) | copy-start | bytes 1179652

commit v3 on v2

--- a/solution.py
+++ b/solution.py
@@ -265,17 +265,17 @@
 
 def fused_kernel(
     n_dp, n_t, n_head, ff,
-    x_ref, cot_ref, seg_ref, gain1_ref, gain2_ref, freq_ref, a_ref, b_ref,
-    out_ref, gin_ref, gains_ref, ga_ref, gb_ref,
+    x_ref, cot_ref, seg_ref, gain1_ref, gain2_ref, freq_ref, wqkv_ref, wout_ref, win_ref, wdown_ref,
+    out_ref, gin_ref, gain1_out, gain2_out, gqkv_ref, gwo_ref, gin_w_ref, gdown_ref,
     xg, cg, ag, bg, n1, n2g, gmg, cosb, sinb, bias, qkvh, probs, hoh, hof, wo, wg, wu, wd,
     rs1s, rs1r, rs2s, rs2r, rs3s, rs3r, rs4s, rs4r, own1, own2, own3, own4,
-    ghf, hid, mix0, mix1, unit2, mid, gmid, ghh, dsb, dqkv, gq, ags, axr, azs, azr, bgs, bxr, bzs, bzr, gpt, gpd,
+    ghf, hid, mix0, mix1, unit2, mid, gmid, ghh, dsb, dqkv, gq, ags, axr, azs, azr, bgs, bxr, bzs, bzr, gpt, gpd, a_ref, b_ref,
     t_send, t_recv, d_send, d_recv,
 ):
     d = lax.axis_index("dp")
     t = lax.axis_index("tensor")
     rows, width = x_ref.shape
-    wrows = a_ref.shape[0]
+    wrows = wout_ref.shape[0]
     head_cols = n_head * HD
     qkv_cols = 3 * head_cols
     span = n_t * rows
@@ -285,11 +285,14 @@
         pl.semaphore_signal(barrier, inc=1, device_id=(d, lax.rem(t + o, n_t)), device_id_type=pl.DeviceIdType.MESH)
     for o in range(1, n_dp):
         pl.semaphore_signal(barrier, inc=1, device_id=(lax.rem(d + o, n_dp), t), device_id_type=pl.DeviceIdType.MESH)
+    a_ref[...] = jnp.concatenate([wqkv_ref[0], wqkv_ref[1], wqkv_ref[2], wout_ref[...]], axis=1)
+    b_pad = jnp.zeros((wrows, b_ref.shape[1] - 3 * ff), BF)
+    b_ref[...] = jnp.concatenate([win_ref[0], win_ref[1], wdown_ref[...], b_pad], axis=1)
     pl.semaphore_wait(barrier, n_t + n_dp - 2)
 
-    def t_copy(stage, src, dst, to, slot):
+    def t_copy(stage, src, dst, to, slot, at=None):
         return pltpu.make_async_remote_copy(
-            src_ref=src, dst_ref=dst, send_sem=t_send.at[stage, to], recv_sem=t_recv.at[stage, slot],
+            src_ref=src, dst_ref=dst, send_sem=t_send.at[stage, to if at is None else at], recv_sem=t_recv.at[stage, slot],
             device_id=(d, to), device_id_type=pl.DeviceIdType.MESH)
 
     xx = lax.rem(d, 2)
@@ -304,15 +307,30 @@
             src_ref=src, dst_ref=dst, send_sem=send, recv_sem=d_recv.at[stage, slot],
             device_id=(to, t), device_id_type=pl.DeviceIdType.MESH)
 
+    over = lax.rem(t + 2, n_t)
+    other = t + 1 - 2 * lax.rem(t, 2)
+
+    def t_relay(stage, buf):
+        t_got(stage, buf, over)
+        far_copy = t_copy(stage, buf.at[over], buf.at[over], other, over, t)
+        far_copy.start()
+
     def t_spread(stage, src, buf):
-        for o in (2, 3, 1)[: n_t - 1]:
-            t_copy(stage, src, buf.at[t], lax.rem(t + o, n_t), t).start()
+        for to in (over, other):
+            t_copy(stage, src, buf.at[t], to, t).start()
 
     def t_got(stage, buf, p):
         t_copy(stage, buf.at[p], buf.at[p], p, p).wait_recv()
 
     def d_got(stage, buf, p):
         d_copy(stage, buf, buf, p, p).wait_recv()
+
+    far = lax.rem(other + 2, n_t)
+
+    def visit(i):
+        first = over * (i % 2) + t * (1 - i % 2)
+        last = far * (i % 2) + other * (1 - i % 2)
+        return first * (1 - i // 2) + last * (i // 2)
 
     def wslice(p):
         return pl.ds(pl.multiple_of(p * wrows, 16), wrows)
@@ -322,8 +340,6 @@
         d_copy(0, a_ref, ag.at[wslice(d)], 2 * z + xx, d).start()
     d_copy(0, a_ref, ag.at[wslice(d)], across, d).start()
     t_spread(1, cot_ref, cg)
-    for z in z_peers:
-        d_copy(1, b_ref, bg.at[wslice(d)], 2 * z + xx, d).start()
     xg[t] = x_ref[...]
     cg[t] = cot_ref[...]
     ag[wslice(d), :] = a_ref[...]
@@ -353,9 +369,13 @@
     gain2 = gain2_ref[...]
 
     def norm_step(i, c):
-        j = lax.rem(t + i, n_t)
-
-        @pl.when(i > 0)
+        j = visit(i)
+
+        @pl.when(i == 1)
+        def _():
+            t_relay(0, xg)
+
+        @pl.when(i > 1)
         def _():
             t_got(0, xg, j)
 
@@ -377,6 +397,8 @@
 
     for z in z_peers:
         pass_on(0, ag, z)
+    for z in z_peers:
+        d_copy(1, b_ref, bg.at[wslice(d)], 2 * z + xx, d).start()
     d_copy(1, b_ref, bg.at[wslice(d)], across, d).start()
     from_across(0, ag)
     wo[...] = ag[:, qkv_cols:]
@@ -455,9 +477,13 @@
     wd[...] = bg[:, 2 * ff:3 * ff]
 
     def hidden_step(i, c):
-        j = lax.rem(t + i, n_t)
-
-        @pl.when(i > 0)
+        j = visit(i)
+
+        @pl.when(i == 1)
+        def _():
+            t_relay(1, cg)
+
+        @pl.when(i > 1)
         def _():
             t_got(1, cg, j)
 
@@ -474,9 +500,13 @@
     t_spread(3, n2g.at[t], n2g)
 
     def ffn_step(i, c):
-        j = lax.rem(t + i, n_t)
-
-        @pl.when(i > 0)
+        j = visit(i)
+
+        @pl.when(i == 1)
+        def _():
+            t_relay(3, n2g)
+
+        @pl.when(i > 1)
         def _():
             t_got(3, n2g, j)
 
@@ -522,7 +552,7 @@
     bgs[:, 3 * ff:] = jnp.zeros((width, bgs.shape[1] - 3 * ff), BF)
 
     def reduce_across(stage, snd, rcv):
-        for z in range(n_z):
+        for z in z_peers + [zz]:
             d_copy(stage, snd.at[wslice(2 * z + 1 - xx)], rcv.at[z], across, z, stage, z).start()
 
     def reduce_along(stage, snd, rcv, sums, got):
@@ -542,9 +572,13 @@
     reduce_across(2, bgs, bxr)
 
     def grad_heads_step(i, c):
-        j = lax.rem(t + i, n_t)
-
-        @pl.when(i > 0)
+        j = visit(i)
+
+        @pl.when(i == 1)
+        def _():
+            t_relay(6, gmg)
+
+        @pl.when(i > 1)
         def _():
             t_got(6, gmg, j)
 
@@ -611,7 +645,8 @@
     unit1, inv1 = rms_parts(x_ref[...].astype(F32))
     gain_attn_part = jnp.sum(grad_one * unit1, axis=0, keepdims=True)
     gpt[t] = jnp.concatenate([gain_attn_part, gain_ffn_part, jnp.zeros((6, width), F32)], axis=0)
-    t_spread(8, gpt.at[t], gpt)
+    for o in range(1, n_t):
+        t_copy(8, gpt.at[t], gpt.at[t], lax.rem(t + o, n_t), t).start()
     gin_ref[...] = gmid[...] + norm_back(grad_one, unit1, inv1, gain1)
     out_ref[...] = (mid[...] + collect(5, own3, rs3r)).astype(BF)
 
@@ -621,18 +656,29 @@
     for o in range(1, n_dp):
         d_copy(4, gpd.at[d], gpd.at[d], lax.rem(d + o, n_dp), d).start()
 
-    gb_ref[...] = reduce_end(2, bgs, bxr, bzr)
-    ga_ref[...] = reduce_end(3, ags, axr, azr)
+    total = reduce_end(2, bgs, bxr, bzr)
+    gin_w_ref[0] = total[:, :ff]
+    gin_w_ref[1] = total[:, ff:2 * ff]
+    gdown_ref[...] = total[:, 2 * ff:3 * ff]
+    total = reduce_end(3, ags, axr, azr)
+    for k in range(3):
+        gqkv_ref[k] = total[:, head_cols * k:head_cols * (k + 1)]
+    gwo_ref[...] = total[:, qkv_cols:]
 
     for o in range(1, n_dp):
         p = lax.rem(d + o, n_dp)
         d_got(4, gpd.at[p], p)
-    gains_ref[...] = jnp.sum(gpd[...], axis=0)
+    gains = jnp.sum(gpd[...], axis=0)
+    gain1_out[...] = gains[0:1]
+    gain2_out[...] = gains[1:2]
 
     for o in range(1, n_t):
         p = lax.rem(t + o, n_t)
-        for stage, ref in enumerate((xg, cg, rs1s, n2g, rs2s, rs3s, gmg, rs4s, gpt)):
+        for stage, ref in ((2, rs1s), (4, rs2s), (5, rs3s), (7, rs4s), (8, gpt)):
             t_copy(stage, ref.at[p], ref.at[p], p, p).wait_send()
+    for stage, ref in ((0, xg), (1, cg), (3, n2g), (6, gmg)):
+        for at in (over, other, t):
+            t_copy(stage, ref.at[over], ref.at[over], other, over, at).wait_send()
 
     def d_sent(lane, ref, at):
         d_copy(0, ref, ref, across, d, lane, at).wait_send()
@@ -665,10 +711,6 @@
     span = n_t * rows
     a_cols = 4 * head_cols
     b_cols = -(-3 * ff // 128) * 128
-    block_a = jnp.concatenate([query_key_value_weight.reshape(wrows, -1), w_out], axis=1)
-    block_b = jnp.concatenate(
-        [w_ffn_in.reshape(wrows, -1), w_ffn_out, jnp.zeros((wrows, b_cols - 3 * ff), BF)], axis=1
-    )
     half = np.arange(32, dtype=np.float64)
     freq = np.tile(THETA ** (-2.0 * half / HD), 4).astype(np.float32)[None]
     vmem = pl.BlockSpec(memory_space=pltpu.VMEM)
@@ -692,38 +734,42 @@
         v((n_head, n_t, rows, HD)), v((n_t, rows, span)), v((3 * n_head, n_t, rows, HD), F32),
         v((n_t, rows, 3 * head_cols)),
         v((width, a_cols)), v(part_a), v(part_a), v(part_a), v((width, b_cols)), v(part_b), v(part_b), v(part_b),
-        v((n_t, 8, width), F32), v((n_dp, 8, width), F32),
+        v((n_t, 8, width), F32), v((n_dp, 8, width), F32), v((wrows, a_cols)), v((wrows, b_cols)),
         pltpu.SemaphoreType.DMA((9, n_t)), pltpu.SemaphoreType.DMA((9, n_t)),
         pltpu.SemaphoreType.DMA((9, n_dp)), pltpu.SemaphoreType.DMA((9, n_dp)),
     ]
-    result, grad_input, gains, grad_a, grad_b = pl.pallas_call(
+    result, grad_input, gain_one, gain_two, grad_qkv, grad_out, grad_in, grad_down = pl.pallas_call(
         functools.partial(fused_kernel, n_dp, n_t, n_head, ff),
         out_shape=(
             jax.ShapeDtypeStruct((rows, width), BF),
             jax.ShapeDtypeStruct((rows, width), F32),
-            jax.ShapeDtypeStruct((8, width), F32),
-            jax.ShapeDtypeStruct((wrows, a_cols), F32),
-            jax.ShapeDtypeStruct((wrows, b_cols), F32),
+            jax.ShapeDtypeStruct((1, width), F32),
+            jax.ShapeDtypeStruct((1, width), F32),
+            jax.ShapeDtypeStruct((3, wrows, head_cols), F32),
+            jax.ShapeDtypeStruct((wrows, head_cols), F32),
+            jax.ShapeDtypeStruct((2, wrows, ff), F32),
+            jax.ShapeDtypeStruct((wrows, ff), F32),
         ),
-        in_specs=[vmem] * 8,
-        out_specs=(vmem,) * 5,
+        in_specs=[vmem] * 10,
+        out_specs=(vmem,) * 8,
         scratch_shapes=scratch,
         compiler_params=pltpu.CompilerParams(
             collective_id=0, has_side_effects=True, vmem_limit_bytes=60 * 1024 * 1024
         ),
         name="fused_layer",
     )(
-        inputs, cotangent, segment_ids, gain_attn[None], gain_ffn[None], jnp.asarray(freq), block_a, block_b,
+        inputs, cotangent, segment_ids, gain_attn[None], gain_ffn[None], jnp.asarray(freq),
+        jnp.swapaxes(query_key_value_weight, 0, 1), w_out, jnp.swapaxes(w_ffn_in, 0, 1), w_ffn_out,
     )
     return (
         result,
         grad_input,
-        gains[0],
-        gains[1],
-        grad_a[:, : 3 * head_cols].reshape(wrows, 3, head_cols),
-        grad_a[:, 3 * head_cols:],
-        grad_b[:, : 2 * ff].reshape(wrows, 2, ff),
-        grad_b[:, 2 * ff:3 * ff],
+        gain_one[0],
+        gain_two[0],
+        jnp.swapaxes(grad_qkv, 0, 1),
+        grad_out,
+        jnp.swapaxes(grad_in, 0, 1),
+        grad_down,
     )
 
 

time: 141 us -> 134 us (0.950)
  Pallas kernels: 126 us -> 121 us
  local copies, waits for them, and re-layouts: 12.4 us -> 9.9 us
    slice x6 -> x0, local copies, waits for them, and re-layouts: 4.95 us -> none  [the longest x1 1.63 us: on_device_fused(): grad_a[:, 3 * head_cols:]]
    unnamed x20 -> x25, local copies, waits for them, and re-layouts: 4.06 us -> 8.74 us
    pallas_call x1, Pallas kernels: 126 us -> 121 us  [on_device_fused(): pl.pallas_call(functools.partial(fused_kernel, n_dp, n_t, n_head, ff), ou...]
    reshape x3 -> x0, local copies, waits for them, and re-layouts: 2.2 us -> none  [the longest x1 1.1 us: on_device_fused(): w_ffn_in.reshape(wrows, -1)]
    concatenate x2 -> x0, other arithmetic: 1.51 us -> none  [the longest x1 0.76 us: on_device_fused(): jnp.concatenate([w_ffn_in.reshape(wrows, -1), w_ffn_out, jnp.zeros((wrows...]
where the time goes in v3:
time: 134 us; the launch traced here: 133 us
  Pallas kernels  121 us (90%)
  local copies, waits for them, and re-layouts  9.9 us (7%)
    pallas_call x1, Pallas kernels, on_device_fused(): pl.pallas_call(functools.partial(fused_kernel, n_dp, n_t, n_head, ff), ou...  121 us
    unnamed x25, local copies, waits for them, and re-layouts  8.74 us

profile of v3, /device:TPU:25, one launch (start us, length us, event | category | flops | bytes accessed | tf_op | source)
XLA Modules:
  0.0 133.0 jit_solution(7911299023873281582)
XLA Ops:
  0.6 0.0 copy-start.5
  0.6 1.6 %copy.21 = bf16[96,2,288]{2,0,1:T(8,128)(2,1)} copy(bf16[96,2,288]{2,1,0:T(2,128)(2,1)} %param.16) | data formatting | bytes 221184 | tf_op args[6]
  2.2 0.0 copy-start.6
  2.2 0.0 copy-done.5
  2.2 0.6 broadcast_in_dim.6.gain1_ref
  2.8 0.1 copy-done.6
  2.9 0.6 broadcast_in_dim.7.gain2_ref
  3.5 121.2 %fused_layer.1 = (bf16[128,768]{1,0:T(8,128)(2,1)}, f32[128,768]{1,0:T(8,128)}, f32[1,768]{1,0:T(1,128)}, f32[1,768]{1,0:T(1,128)}, f32[3,96,192]{2,1,0:T(8,128)...) custom-call(bf16[128,768]{1,0:T(8,128)(2,1)} %x_ref.1, bf16[128,768]{1,0:T(8,128)(2,1)} %cot_ref.1, ...), custom_call_target="tpu_custom_call" | custom-call | tf_op jit(solution)/shard_map/fused_layer/pallas_call | solution.py:741
  124.7 0.0 copy-start.2
  124.7 0.0 copy-start
  124.7 2.0 %copy.19 = f32[96,2,288]{2,1,0:T(2,128)} copy(f32[96,2,288]{2,0,1:T(8,128)} %bitcast.8) | data formatting | bytes 442368
  126.7 0.0 copy-start.8
  126.7 0.7 copy-done.8
  127.3 0.0 copy-start.7
  127.3 0.6 reduce
  127.9 0.1 copy-done.7
  128.0 0.6 reduce.1
  128.6 0.0 copy-done.2
  128.6 0.7 copy.27
  129.3 0.0 copy-done
  129.3 0.0 copy-start.1
  129.3 0.7 copy.28
  130.0 0.4 copy-done.1
  130.4 0.0 copy-start.4
  130.4 0.7 copy.29
  131.1 0.2 copy-done.4
  131.3 0.0 copy-start.3
  131.4 0.6 copy.30
  132.0 0.3 copy-done.3
  132.3 0.7 copy.31
Async XLA Ops:
  0.6 1.6 %copy-start.5 = (f32[768]{0:T(1024)S(1)}, f32[768]{0:T(1024)}, u32[]{:S(2)}) copy-start(f32[768]{0:T(1024)} %param.12) | copy-start | bytes 9220
  2.2 0.7 copy-start.6
  124.7 3.9 %copy-start.2 = (bf16[128,768]{1,0:T(8,128)(2,1)S(1)}, bf16[128,768]{1,0:T(8,128)(2,1)}, u32[]{:S(2)}) copy-start(bf16[128,768]{1,0:T(8,128)(2,1)} %get-tuple-element.40) | copy-start | bytes 589828
  124.7 4.6 %copy-start = (f32[128,768]{1,0:T(8,128)S(1)}, f32[128,768]{1,0:T(8,128)}, u32[]{:S(2)}) copy-start(f32[128,768]{1,0:T(8,128)} %get-tuple-element.41) | copy-start | bytes 1179652
  126.7 0.7 copy-start.8
  127.3 0.7 copy-start.7
  129.3 1.1 copy-start.1
  130.4 1.0 copy-start.4
  131.3 0.9 copy-start.3
